TPU v7x, 256 devices: a whole 4x4x8 slice. The times are simulated.
256 devices in a mesh: rep: 16 (over z, y_lo), fsdp: 16 (over y_hi, x, core).
Axes of the slice: x: 4, y: 4 (y_hi: 2, y_lo: 2; y = y_hi * 2 + y_lo), z: 8, core: 2. Of those that a mesh axis runs over, the one named last changes fastest.
Arguments:
- param: float32 [16, 512, 8192], P('rep', 'fsdp'), may hold values from -6 to 6
- first: float32 [16, 512, 8192], P('rep', 'fsdp'), may hold values from -6 to 6
- second: float32 [16, 512, 8192], P('rep', 'fsdp'), may hold values from 0.5 to 4
- push_weight: float32 [16], P('rep'), may hold values from 0.5 to 2
- acts: bfloat16 [16, 6144, 8192], P('rep', 'fsdp'), may hold values from -6 to 6
- cotangent: bfloat16 [16, 6144, 512], P('rep', 'fsdp'), may hold values from -0.078125 to 0.078125
- exponent: int32 [1], replicated, may hold values from 0 to 3
Outputs:
- mixed_param: float32 [16, 512, 8192], P('rep', 'fsdp')
- new_first: float32 [16, 512, 8192], P('rep', 'fsdp')
- new_second: float32 [16, 512, 8192], P('rep', 'fsdp')
- mixed_weight: float32 [16], P('rep')
All inputs are finite; a program needn't handle non-finite values.
Results may differ from a plain program's by a relative error of at most 0.0003.
Values sent between devices are 32-bit elements; how exact they have to be, the bound alone decides.
No kernel may reach another device: no remote copies, remote signals or barrier semaphores. Data moves between devices by JAX's collectives and lax.ppermute only.
A program may use at most 128 MiB of HBM per device.

v0:
```python
from functools import partial

import jax
import jax.numpy as jnp
from jax import lax
from jax.experimental import pallas as pl
from jax.experimental.pallas import tpu as pltpu
from jax.sharding import PartitionSpec as P

X_WIDTH = 4096
Y_WIDTH = 4096
PIECE = 2048
LIMIT = 32 * 1024 * 1024
ANY = pl.BlockSpec(memory_space=pl.ANY)


def call(kernel, width, tile, ins, outs, after=(), aliases=None, cost=1, limit=LIMIT):
    specs, operands = [], []
    for array, start in ins:
        rows, columns = array.shape
        operands.append(array)
        if start is None:
            specs.append(pl.BlockSpec((rows, columns), lambda j: (0, 0)))
        else:
            specs.append(pl.BlockSpec((rows, tile), lambda j, s=start // tile: (0, j + s)))
    out_specs, shapes = [], []
    for rows, columns, start in outs:
        out_specs.append(pl.BlockSpec((rows, tile), lambda j, s=start // tile: (0, j + s)))
        shapes.append(jax.ShapeDtypeStruct((rows, columns), jnp.float32))
    count, skipped = len(ins), len(after)
    pairs = {}
    for out, array in (aliases or {}).items():
        pairs[count + skipped + len(pairs)] = out
    extra = list(after) + list((aliases or {}).values())

    def wrapped(*refs):
        kernel(*refs[:count], *refs[count + len(extra) :])

    return pl.pallas_call(
        wrapped,
        grid=(width // tile,),
        in_specs=specs + [ANY] * len(extra),
        out_specs=out_specs,
        out_shape=shapes,
        input_output_aliases=pairs,
        compiler_params=pltpu.CompilerParams(vmem_limit_bytes=limit),
        cost_estimate=pl.CostEstimate(flops=0, bytes_accessed=cost * 3_000_000, transcendentals=0),
    )(*operands, *extra)


def strips(rows, step, work):
    def one(i, carry):
        work(pl.ds(pl.multiple_of(i * step, step), step))
        return carry

    lax.fori_loop(0, rows // step, one, 0)


def product(cot, acts, start, width, after=(), limit=LIMIT):
    rows, tokens = cot.shape

    def kernel(c_ref, a_ref, o_ref):
        o_ref[...] = jnp.dot(c_ref[...], a_ref[...], preferred_element_type=jnp.float32)

    return call(
        kernel, width, 1024, [(cot, None), (acts, start)], [(rows, width, 0)], after, limit=limit
    )[0]


def product_add(
    cot, acts, peer, start, kind, after, whole, out_start, held=None
):
    rows, tokens = cot.shape

    def kernel(c_ref, a_ref, p_ref, *o_refs):
        total = jnp.dot(c_ref[...], a_ref[...], preferred_element_type=jnp.float32) + p_ref[...]
        if kind == "y":
            o_refs[0][...] = total[:128]
            o_refs[1][...] = total[128:]
        else:
            for d in range(4):
                o_refs[d][:32] = total[32 * d : 32 * d + 32]
                o_refs[d][32:] = total[128 + 32 * d : 160 + 32 * d]

    outs = [(128, whole, out_start)] * 2 if kind == "y" else [(64, whole, out_start)] * 4
    return call(
        kernel, peer.shape[1], 1024, [(cot, None), (acts, start), (peer, 0)], outs, after,
        dict(enumerate(held)) if held else None,
    )


def add_split(own, peer, after, whole, out_start, held=None):
    width = own.shape[1]

    def kernel(a_ref, b_ref, *o_refs):
        for d in range(4):
            def work(at, d=d):
                from_at = pl.ds(at.start + 32 * d, at.size)
                o_refs[d][at] = a_ref[from_at] + b_ref[from_at]

            strips(32, 8, work)

    return call(
        kernel, width, 2048, [(own, 0), (peer, 0)], [(32, whole, out_start)] * 4, after,
        dict(enumerate(held)) if held else None,
    )


def sum_split(terms, after=()):
    width = terms[0].shape[1]

    def kernel(a_ref, b_ref, c_ref, d_ref, *o_refs):
        for i in range(2):
            def work(at, i=i):
                from_at = pl.ds(at.start + 32 * i, at.size)
                o_refs[i][at] = (a_ref[from_at] + b_ref[from_at]) + (c_ref[from_at] + d_ref[from_at])

            strips(32, 8, work)

    return call(kernel, width, 2048, [(t, 0) for t in terms], [(32, width, 0)] * 2, after, None, 30)


def adam(terms, param, first, second, held, start, width, whole, step_start, after=()):
    count, columns = len(terms), param.shape[1]

    def kernel(*refs):
        param_ref, first_ref, second_ref = refs[count : count + 3]
        step_ref, new_first_ref, new_second_ref = refs[-3:]

        def work(at):
            grad = refs[0][at]
            for ref in refs[1:count]:
                grad = grad + ref[at]
            new_first = 0.9 * first_ref[at] + 0.1 * grad
            new_second = 0.999 * second_ref[at] + 0.001 * grad * grad
            new_first_ref[at] = new_first
            new_second_ref[at] = new_second
            step_ref[at] = param_ref[at] - 0.1 * (new_first / (jnp.sqrt(new_second) + 1e-08))

        strips(32, 8, work)

    ins = [(t, 0) for t in terms] + [(a, start) for a in (param, first, second)]
    outs = [(32, whole, step_start), (32, columns, start), (32, columns, start)]
    return call(kernel, width, 2048, ins, outs, after, held)


def to_core(value):
    return lax.ppermute(value, "fsdp", [(i, i ^ 1) for i in range(16)])


def to_y(value):
    return lax.ppermute(value, "fsdp", [(i, i ^ 8) for i in range(16)])


def to_x(value, by):
    return lax.ppermute(
        value, "fsdp", [(i, (i & 9) | ((((i >> 1) + by) & 3) << 1)) for i in range(16)]
    )


def to_rep(value, by):
    return lax.ppermute(value, "rep", [(i, (i + by) % 16) for i in range(16)])


def dealt(cot):
    me = lax.axis_index("fsdp")
    at = lax.broadcasted_iota(jnp.int32, (512, 512), 0)
    rel = lax.broadcasted_iota(jnp.int32, (512, 512), 1)
    to = rel >> 5
    core = (me ^ 1 ^ (to >> 3)) & 1
    y = ((me >> 3) ^ (to >> 2)) & 1
    x = ((me >> 1) + to) & 3
    source = (y * 8 + x * 2 + core) * 32 + (rel & 31)
    pick = (at == source).astype(cot.dtype)
    return lax.dot_general(
        pick, cot, (((0,), (1,)), ((), ())), preferred_element_type=jnp.float32
    ).astype(cot.dtype)


def pushed(operands, power):
    return [to_rep(value, 2**power) for value in operands]


def push(exponent, operands):
    return lax.switch(exponent, [partial(pushed, power=p) for p in range(4)], operands)


def body(param, first, second, push_weight, acts, cotangent, exponent):
    cot = dealt(cotangent[0])
    theirs, mine = cot[:256], cot[256:]
    param, first, second, acts = param[0], first[0], second[0], acts[0]
    columns = param.shape[1]
    order = (1, 3, 2)

    cuts = range(0, columns, PIECE)
    outs, ins = [], []
    for start in cuts:
        outs.append(product(theirs, acts, start, PIECE, outs[-1:]))
        ins.append(to_core(outs[-1]))
    parts_x, after = None, outs[-1:]
    for start in cuts[: X_WIDTH // PIECE]:
        parts_x = product_add(
            mine, acts, ins[start // PIECE], start, "x", after, X_WIDTH, start, parts_x
        )
        after = []
    sum_x = [to_x(parts_x[d], d) for d in order]
    after, parts_y, peer_y = parts_x[:1], [], []
    for start in cuts[X_WIDTH // PIECE :]:
        parts_y.append(
            product_add(mine, acts, ins[start // PIECE], start, "y", after, PIECE, 0)
        )
        after = parts_y[-1][:1]
        peer_y.append(to_y(parts_y[-1][1]))

    halves_x = sum_split([parts_x[0]] + sum_x, after)
    last_x = to_y(halves_x[1])
    blocks_y, after = None, halves_x[:1]
    for i, (parts, peer) in enumerate(zip(parts_y, peer_y)):
        blocks_y = add_split(parts[0], peer, after, Y_WIDTH, i * PIECE, blocks_y)
        after = []
    last_y = [to_x(blocks_y[d], d) for d in order]
    step_x, new_first, new_second = adam(
        [halves_x[0], last_x], param, first, second, None, 0, X_WIDTH, X_WIDTH, 0, [blocks_y[0]]
    )
    peer_x, weight_peer = push(exponent[0], (step_x, push_weight))
    step_y, new_first, new_second = adam(
        [blocks_y[0]] + last_y, param, first, second, {1: new_first, 2: new_second},
        X_WIDTH, Y_WIDTH, Y_WIDTH, 0, [peer_x],
    )
    (peer_y,) = push(exponent[0], (step_y,))
    mixed = jnp.concatenate(
        [0.5 * step_x + 0.5 * peer_x, 0.5 * step_y + 0.5 * peer_y], axis=1
    )
    weight = 0.5 * push_weight + 0.5 * weight_peer
    return mixed[None], new_first[None], new_second[None], weight


def solution(mesh):
    return jax.shard_map(
        body,
        mesh=mesh,
        in_specs=(
            P("rep", "fsdp", None),
            P("rep", "fsdp", None),
            P("rep", "fsdp", None),
            P("rep"),
            P("rep", "fsdp", None),
            P("rep", "fsdp", None),
            P(),
        ),
        out_specs=(
            P("rep", "fsdp", None),
            P("rep", "fsdp", None),
            P("rep", "fsdp", None),
            P("rep"),
        ),
        check_vma=False,
    )
```

profile of v0, /device:TPU:16, one launch (start us, length us, event | category | flops | bytes accessed | tf_op | source)
XLA Modules:
  0.0 126.4 jit_solution(3010975762387903057)
XLA Ops:
  2.2 2.8 %copy-done.1 = bf16[1,384,8192]{2,1,0:T(8,128)(2,1)S(1)} copy-done((bf16[1,384,8192]{2,1,0:T(8,128)(2,1)S(1)}, bf16[1,384,8192]{2,1,0:T(8,128)(2,1)}, u32[]{:S(2)}) %copy-start.1) | copy-done | bytes 6291480
  11.0 1.3 %shard_map.106 = (f32[64,4096]{1,0:T(8,128)S(1)}, f32[64,4096]{1,0:T(8,128)S(1)}, f32[64,4096]{1,0:T(8,128)S(1)}, f32[64,4096]{1,0:T(8,128)S(1)}) custom-call(bf16[256,384]{1,0:T(8,128)(2,1)S(1)} %get-tuple-element.98.refs_0_, bf16[384,8192]{1,0:T(8,128)(2,1)S(1)} %bitcast.18, f32[256,2048]{1,0:T(8,128)S(1)} %collective-permute-done.13.refs_2_, ...), custom_call_target="tpu_custom_call" | custom-call | bytes 3000000 | tf_op jit(solution)/shard_map/pallas_call | solution.py:39
  12.3 4.0 %collective-permute-done.12.refs_2_ = f32[256,2048]{1,0:T(8,128)S(1)} collective-permute-done((f32[256,2048]{1,0:T(8,128)S(1)}, f32[256,2048]{1,0:T(8,128)S(1)}, u32[]{:S(2)}, u32[]{:S(2)}) %collective-permute-start.12) | collective-permute-done | bytes 2097184 | tf_op jit(solution)/shard_map/ppermute | solution.py:148
  16.3 1.3 %shard_map.107 = (f32[64,4096]{1,0:T(8,128)S(1)}, f32[64,4096]{1,0:T(8,128)S(1)}, f32[64,4096]{1,0:T(8,128)S(1)}, f32[64,4096]{1,0:T(8,128)S(1)}) custom-call(bf16[256,384]{1,0:T(8,128)(2,1)S(1)} %get-tuple-element.98.refs_0_, bf16[384,8192]{1,0:T(8,128)(2,1)S(1)} %bitcast.19, ...), custom_call_target="tpu_custom_call", output_to_operand_aliasing={{0}: (3, {}), {1}: (4, {}), {2}: (5, {}), {3}: (6, {})} | custom-call | bytes 3000000 | tf_op jit(solution)/shard_map/pallas_call | solution.py:39
  17.7 1.6 %collective-permute-start.14 = (f32[64,4096]{1,0:T(8,128)S(1)}, f32[64,4096]{1,0:T(8,128)S(1)}, u32[]{:S(2)}, u32[]{:S(2)}) collective-permute-start(f32[64,4096]{1,0:T(8,128)S(1)} %get-tuple-element.72), channel_id=1, source_target_pairs={{0,2},{1,3},{2,4},{3,5},{4,6},{5,7},{6,0},{7,1},{8,10},{9,11},{10,... | collective-permute-start | bytes 3145736 | tf_op jit(solution)/shard_map/ppermute | solution.py:156
  19.2 1.8 %collective-permute-start.15 = (f32[64,4096]{1,0:T(8,128)S(1)}, f32[64,4096]{1,0:T(8,128)S(1)}, u32[]{:S(2)}, u32[]{:S(2)}) collective-permute-start(f32[64,4096]{1,0:T(8,128)S(1)} %get-tuple-element.73), channel_id=1, source_target_pairs={{0,6},{1,7},{2,0},{3,1},{4,2},{5,3},{6,4},{7,5},{8,14},{9,15},{10,... | collective-permute-start | bytes 3145736 | tf_op jit(solution)/shard_map/ppermute | solution.py:156
  21.0 1.8 %collective-permute-start.16 = (f32[64,4096]{1,0:T(8,128)S(1)}, f32[64,4096]{1,0:T(8,128)S(1)}, u32[]{:S(2)}, u32[]{:S(2)}) collective-permute-start(f32[64,4096]{1,0:T(8,128)S(1)} %get-tuple-element.74), channel_id=1, source_target_pairs={{0,4},{1,5},{2,6},{3,7},{4,0},{5,1},{6,2},{7,3},{8,12},{9,13},{10,... | collective-permute-start | bytes 3145736 | tf_op jit(solution)/shard_map/ppermute | solution.py:156
  22.8 2.3 %shard_map.108 = (f32[128,2048]{1,0:T(8,128)S(1)}, f32[128,2048]{1,0:T(8,128)S(1)}) custom-call(bf16[256,384]{1,0:T(8,128)(2,1)S(1)} %get-tuple-element.98.refs_0_, bf16[384,8192]{1,0:T(8,128)(2,1)S(1)} %bitcast.20, f32[256,2048]{1,0:T(8,128)} %collective-permute-done.18.refs_2_, f32[64,4096]{1,0:T(8,128)S(1)} %get-tuple-element.71.refs_3_.refs_0_), custom_call_target="tpu_custom_call" | custom-call | bytes 3000000 | tf_op jit(solution)/shard_map/pallas_call | solution.py:39
  25.5 1.3 %shard_map.109 = (f32[128,2048]{1,0:T(8,128)S(1)}, f32[128,2048]{1,0:T(8,128)S(1)}) custom-call(bf16[256,384]{1,0:T(8,128)(2,1)S(1)} %get-tuple-element.98.refs_0_, bf16[384,8192]{1,0:T(8,128)(2,1)S(1)} %bitcast.21, f32[256,2048]{1,0:T(8,128)S(1)} %collective-permute-done.17.refs_2_, f32[128,2048]{1,0:T(8,128)S(1)} %get-tuple-element.75.refs_3_.refs_0_), custom_call_target="tpu_custom_call" | custom-call | bytes 3000000 | tf_op jit(solution)/shard_map/pallas_call | solution.py:39
  26.8 3.3 %collective-permute-start.20 = (f32[128,2048]{1,0:T(8,128)S(1)}, f32[128,2048]{1,0:T(8,128)S(1)}, u32[]{:S(2)}, u32[]{:S(2)}) collective-permute-start(f32[128,2048]{1,0:T(8,128)S(1)} %get-tuple-element.79), channel_id=1, source_target_pairs={{0,8},{1,9},{2,10},{3,11},{4,12},{5,13},{6,14},{7,15},{8,0},{9,1},... | collective-permute-start | bytes 3145736 | tf_op jit(solution)/shard_map/ppermute | solution.py:152
  30.1 14.0 %collective-permute-done.14.refs_1_ = f32[64,4096]{1,0:T(8,128)S(1)} collective-permute-done((f32[64,4096]{1,0:T(8,128)S(1)}, f32[64,4096]{1,0:T(8,128)S(1)}, u32[]{:S(2)}, u32[]{:S(2)}) %collective-permute-start.14) | collective-permute-done | bytes 1048608 | tf_op jit(solution)/shard_map/ppermute | solution.py:156
  45.3 22.3 %collective-permute-done.16.refs_3_ = f32[64,4096]{1,0:T(8,128)S(1)} collective-permute-done((f32[64,4096]{1,0:T(8,128)S(1)}, f32[64,4096]{1,0:T(8,128)S(1)}, u32[]{:S(2)}, u32[]{:S(2)}) %collective-permute-start.16) | collective-permute-done | bytes 1048608 | tf_op jit(solution)/shard_map/ppermute | solution.py:156
  71.8 3.4 %collective-permute-done.20.refs_1_ = f32[128,2048]{1,0:T(8,128)S(1)} collective-permute-done((f32[128,2048]{1,0:T(8,128)S(1)}, f32[128,2048]{1,0:T(8,128)S(1)}, u32[]{:S(2)}, u32[]{:S(2)}) %collective-permute-start.20) | collective-permute-done | bytes 1048608 | tf_op jit(solution)/shard_map/ppermute | solution.py:152
  76.6 2.9 %collective-permute-start.23 = (f32[32,4096]{1,0:T(8,128)}, f32[32,4096]{1,0:T(8,128)}, u32[]{:S(2)}, u32[]{:S(2)}) collective-permute-start(f32[32,4096]{1,0:T(8,128)} %get-tuple-element.89), channel_id=1, source_target_pairs={{0,6},{1,7},{2,0},{3,1},{4,2},{5,3},{6,4},{7,5},{8,14},{9,15},{10,... | collective-permute-start | bytes 1572872 | tf_op jit(solution)/shard_map/ppermute | solution.py:156
  80.0 4.7 %collective-permute-done.19.refs_1_ = f32[32,4096]{1,0:T(8,128)S(1)} collective-permute-done((f32[32,4096]{1,0:T(8,128)S(1)}, f32[32,4096]{1,0:T(8,128)S(1)}, u32[]{:S(2)}, u32[]{:S(2)}) %collective-permute-start.19) | collective-permute-done | bytes 524320 | tf_op jit(solution)/shard_map/ppermute | solution.py:152
  84.8 1.6 %shard_map.113 = (f32[32,4096]{1,0:T(8,128)S(1)}, f32[32,8192]{1,0:T(8,128)}, f32[32,8192]{1,0:T(8,128)}) custom-call(f32[32,4096]{1,0:T(8,128)S(1)} %get-tuple-element.77.refs_2_.refs_0_, f32[32,4096]{1,0:T(8,128)S(1)} %collective-permute-done.19.refs_1_, f32[32,8192]{1,0:T(8,128)S(1)} %bitcast.22, f32[32,8192]{1,0:T(8,128)S(1)} %bitcast.24, ...), custom_call_target="tpu_custom_call" | custom-call | bytes 3000000 | tf_op jit(solution)/shard_map/pallas_call | solution.py:39
  87.1 16.7 %conditional.2 = (f32[32,4096]{1,0:T(8,128)}, f32[1]{0:T(128)}) conditional(s32[]{:T(128)} %bitcast.5, (f32[32,4096]{1,0:T(8,128)S(1)}, f32[1]{0:T(128)}) %tuple.36, (f32[32,4096]{1,0:T(8,128)S(1)}, f32[1]{0:T(128)}) %tuple.36, (f32[32,4096]{1,0:T(8,128)S(1)}, f32[1]{0:T(128)}) %tuple.36, (f32[32,4096]{1,0:T(8,128)S(1)}, ...), branch_computations={%region_0.0_spmd, %region_1.0_spmd, %region_2.0_spmd, %region_3.0_... | conditional | bytes 2097264 | solution.py:185
  87.1 1.9 %collective-permute-start.2 = (f32[32,4096]{1,0:T(8,128)S(1)}, f32[32,4096]{1,0:T(8,128)}, u32[]{:S(2)}, u32[]{:S(2)}) collective-permute-start(f32[32,4096]{1,0:T(8,128)S(1)} %get-tuple-element.27), channel_id=1, source_target_pairs={{0,32},{16,48},{32,64},{48,80},{64,96},{80,112},{96,128},{112,144}... | collective-permute-start | bytes 1572872 | tf_op jit(solution)/shard_map/cond/branch_1_fun/ppermute | solution.py:162
  89.0 1.9 %collective-permute-start.3 = (f32[1]{0:T(128)}, f32[1]{0:T(128)}, u32[]{:S(2)}, u32[]{:S(2)}) collective-permute-start(f32[1]{0:T(128)} %get-tuple-element.28), channel_id=1, source_target_pairs={{0,32},{16,48},{32,64},{48,80},{64,96},{80,112},{96,128},{112,144}... | collective-permute-start | bytes 20 | tf_op jit(solution)/shard_map/cond/branch_1_fun/ppermute | solution.py:162
  91.0 12.8 %collective-permute-done.3 = f32[1]{0:T(128)} collective-permute-done((f32[1]{0:T(128)}, f32[1]{0:T(128)}, u32[]{:S(2)}, u32[]{:S(2)}) %collective-permute-start.3) | collective-permute-done | bytes 36 | tf_op jit(solution)/shard_map/cond/branch_1_fun/ppermute | solution.py:162
  103.8 2.1 %add_multiply_fusion.1 = f32[32,4096]{1,0:T(8,128)} fusion(f32[32,4096]{1,0:T(8,128)} %copy-done.7, f32[32,4096]{1,0:T(8,128)} %get-tuple-element.87.refs_7_), kind=kLoop, calls=%fused_computation.5 | loop fusion | flops 262144 | bytes 1572864 | tf_op jit(solution)/shard_map/add | solution.py:232
  106.0 2.6 %shard_map.114 = (f32[32,4096]{1,0:T(8,128)S(1)}, f32[32,8192]{1,0:T(8,128)}, f32[32,8192]{1,0:T(8,128)}) custom-call(f32[32,4096]{1,0:T(8,128)S(1)} %get-tuple-element.85.refs_5_.refs_0_, f32[32,4096]{1,0:T(8,128)} %collective-permute-done.22.refs_1_, f32[32,4096]{1,0:T(8,128)} %collective-permute-done.23.refs_2_, ...), custom_call_target="tpu_custom_call", output_to_operand_aliasing={{1}: (8, {}), {2}: (9, {})} | custom-call | bytes 3000000 | tf_op jit(solution)/shard_map/pallas_call | solution.py:39
  109.4 13.0 %conditional.3 = (f32[32,4096]{1,0:T(8,128)}) conditional(s32[]{:T(128)} %bitcast.5, f32[32,4096]{1,0:T(8,128)S(1)} %get-tuple-element.93, f32[32,4096]{1,0:T(8,128)S(1)} %get-tuple-element.93, f32[32,4096]{1,0:T(8,128)S(1)} %get-tuple-element.93, f32[32,4096]{1,0:T(8,128)S(1)} %get-tuple-element.93), branch_computations={%region_4.0_spmd, %region_5.0_spmd, %region_6.0_spmd, %region_7.0_... | conditional | bytes 2097200 | solution.py:185
  109.4 13.0 %collective-permute-done.9 = f32[32,4096]{1,0:T(8,128)} collective-permute-done((f32[32,4096]{1,0:T(8,128)S(1)}, f32[32,4096]{1,0:T(8,128)}, u32[]{:S(2)}, u32[]{:S(2)}) %collective-permute-start.9) | collective-permute-done | bytes 524320 | tf_op jit(solution)/shard_map/cond/branch_1_fun/ppermute | solution.py:162
  (52 shorter events, 17.9 us)
Async XLA Ops:
  2.2 2.8 %copy-start.1 = (bf16[1,384,8192]{2,1,0:T(8,128)(2,1)S(1)}, bf16[1,384,8192]{2,1,0:T(8,128)(2,1)}, u32[]{:S(2)}) copy-start(bf16[1,384,8192]{2,1,0:T(8,128)(2,1)} %param.19) | copy-start | bytes 18874372
  6.1 4.8 %collective-permute-start.13 = (f32[256,2048]{1,0:T(8,128)S(1)}, f32[256,2048]{1,0:T(8,128)S(1)}, u32[]{:S(2)}, u32[]{:S(2)}) collective-permute-start(f32[256,2048]{1,0:T(8,128)S(1)} %shard_map.102.refs_2_), channel_id=1, source_target_pairs={{0,1},{1,0},{2,3},{3,2},{4,5},{5,4},{6,7},{7,6},{8,9},{9,8},{10,11... | collective-permute-start | bytes 6291464 | tf_op jit(solution)/shard_map/ppermute | solution.py:148
  7.4 9.0 %collective-permute-start.12 = (f32[256,2048]{1,0:T(8,128)S(1)}, f32[256,2048]{1,0:T(8,128)S(1)}, u32[]{:S(2)}, u32[]{:S(2)}) collective-permute-start(f32[256,2048]{1,0:T(8,128)S(1)} %shard_map.103.refs_2_), channel_id=1, source_target_pairs={{0,1},{1,0},{2,3},{3,2},{4,5},{5,4},{6,7},{7,6},{8,9},{9,8},{10,11... | collective-permute-start | bytes 6291464 | tf_op jit(solution)/shard_map/ppermute | solution.py:148
  7.9 3.0 %slice-start = ((s8[6291456]{0:T(1024)(128)(4,1)}), s8[4194304]{0:T(1024)(128)(4,1)S(1)}, s32[]{:S(2)}) async-start(s8[6291456]{0:T(1024)(128)(4,1)} %bitcast.16), calls=%async_computation | async-start | bytes 8388608
  9.1 2.0 %slice-start.1 = ((s8[6291456]{0:T(1024)(128)(4,1)}), s8[2097152]{0:T(1024)(128)(4,1)S(1)}, s32[]{:S(2)}) async-start(s8[6291456]{0:T(1024)(128)(4,1)} %bitcast.16), calls=%async_computation.1 | async-start | bytes 4194304
  9.1 13.7 %collective-permute-start.18 = (f32[256,2048]{1,0:T(8,128)S(1)}, f32[256,2048]{1,0:T(8,128)}, u32[]{:S(2)}, u32[]{:S(2)}) collective-permute-start(f32[256,2048]{1,0:T(8,128)S(1)} %shard_map.104.refs_2_), channel_id=1, source_target_pairs={{0,1},{1,0},{2,3},{3,2},{4,5},{5,4},{6,7},{7,6},{8,9},{9,8},{10,11... | collective-permute-start | bytes 6291464 | tf_op jit(solution)/shard_map/ppermute | solution.py:148
  10.4 15.2 %collective-permute-start.17 = (f32[256,2048]{1,0:T(8,128)S(1)}, f32[256,2048]{1,0:T(8,128)S(1)}, u32[]{:S(2)}, u32[]{:S(2)}) collective-permute-start(f32[256,2048]{1,0:T(8,128)S(1)} %shard_map.105.refs_3_), channel_id=1, source_target_pairs={{0,1},{1,0},{2,3},{3,2},{4,5},{5,4},{6,7},{7,6},{8,9},{9,8},{10,11... | collective-permute-start | bytes 6291464 | tf_op jit(solution)/shard_map/ppermute | solution.py:148
  17.7 26.5 %collective-permute-start.14 = (f32[64,4096]{1,0:T(8,128)S(1)}, f32[64,4096]{1,0:T(8,128)S(1)}, u32[]{:S(2)}, u32[]{:S(2)}) collective-permute-start(f32[64,4096]{1,0:T(8,128)S(1)} %get-tuple-element.72), channel_id=1, source_target_pairs={{0,2},{1,3},{2,4},{3,5},{4,6},{5,7},{6,0},{7,1},{8,10},{9,11},{10,... | collective-permute-start | bytes 3145736 | tf_op jit(solution)/shard_map/ppermute | solution.py:156
  19.2 26.0 %collective-permute-start.15 = (f32[64,4096]{1,0:T(8,128)S(1)}, f32[64,4096]{1,0:T(8,128)S(1)}, u32[]{:S(2)}, u32[]{:S(2)}) collective-permute-start(f32[64,4096]{1,0:T(8,128)S(1)} %get-tuple-element.73), channel_id=1, source_target_pairs={{0,6},{1,7},{2,0},{3,1},{4,2},{5,3},{6,4},{7,5},{8,14},{9,15},{10,... | collective-permute-start | bytes 3145736 | tf_op jit(solution)/shard_map/ppermute | solution.py:156
  21.0 46.6 %collective-permute-start.16 = (f32[64,4096]{1,0:T(8,128)S(1)}, f32[64,4096]{1,0:T(8,128)S(1)}, u32[]{:S(2)}, u32[]{:S(2)}) collective-permute-start(f32[64,4096]{1,0:T(8,128)S(1)} %get-tuple-element.74), channel_id=1, source_target_pairs={{0,4},{1,5},{2,6},{3,7},{4,0},{5,1},{6,2},{7,3},{8,12},{9,13},{10,... | collective-permute-start | bytes 3145736 | tf_op jit(solution)/shard_map/ppermute | solution.py:156
  25.1 45.7 %collective-permute-start.21 = (f32[128,2048]{1,0:T(8,128)S(1)}, f32[128,2048]{1,0:T(8,128)S(1)}, u32[]{:S(2)}, u32[]{:S(2)}) collective-permute-start(f32[128,2048]{1,0:T(8,128)S(1)} %get-tuple-element.80), channel_id=1, source_target_pairs={{0,8},{1,9},{2,10},{3,11},{4,12},{5,13},{6,14},{7,15},{8,0},{9,1},... | collective-permute-start | bytes 3145736 | tf_op jit(solution)/shard_map/ppermute | solution.py:152
  26.8 48.3 %collective-permute-start.20 = (f32[128,2048]{1,0:T(8,128)S(1)}, f32[128,2048]{1,0:T(8,128)S(1)}, u32[]{:S(2)}, u32[]{:S(2)}) collective-permute-start(f32[128,2048]{1,0:T(8,128)S(1)} %get-tuple-element.79), channel_id=1, source_target_pairs={{0,8},{1,9},{2,10},{3,11},{4,12},{5,13},{6,14},{7,15},{8,0},{9,1},... | collective-permute-start | bytes 3145736 | tf_op jit(solution)/shard_map/ppermute | solution.py:152
  68.3 16.4 %collective-permute-start.19 = (f32[32,4096]{1,0:T(8,128)S(1)}, f32[32,4096]{1,0:T(8,128)S(1)}, u32[]{:S(2)}, u32[]{:S(2)}) collective-permute-start(f32[32,4096]{1,0:T(8,128)S(1)} %get-tuple-element.78), channel_id=1, source_target_pairs={{0,8},{1,9},{2,10},{3,11},{4,12},{5,13},{6,14},{7,15},{8,0},{9,1},... | collective-permute-start | bytes 1572872 | tf_op jit(solution)/shard_map/ppermute | solution.py:152
  75.2 9.6 %copy-start.2 = (f32[1,32,8192]{2,1,0:T(8,128)S(1)}, f32[1,32,8192]{2,1,0:T(8,128)}, u32[]{:S(2)}) copy-start(f32[1,32,8192]{2,1,0:T(8,128)} %param.15) | copy-start | bytes 3145732
  75.2 9.6 %copy-start.3 = (f32[1,32,8192]{2,1,0:T(8,128)S(1)}, f32[1,32,8192]{2,1,0:T(8,128)}, u32[]{:S(2)}) copy-start(f32[1,32,8192]{2,1,0:T(8,128)} %param.16) | copy-start | bytes 3145732
  75.2 9.6 %copy-start.4 = (f32[1,32,8192]{2,1,0:T(8,128)S(1)}, f32[1,32,8192]{2,1,0:T(8,128)}, u32[]{:S(2)}) copy-start(f32[1,32,8192]{2,1,0:T(8,128)} %param.17) | copy-start | bytes 3145732
  76.2 29.8 %collective-permute-start.22 = (f32[32,4096]{1,0:T(8,128)S(1)}, f32[32,4096]{1,0:T(8,128)}, u32[]{:S(2)}, u32[]{:S(2)}) collective-permute-start(f32[32,4096]{1,0:T(8,128)S(1)} %get-tuple-element.88), channel_id=1, source_target_pairs={{0,2},{1,3},{2,4},{3,5},{4,6},{5,7},{6,0},{7,1},{8,10},{9,11},{10,... | collective-permute-start | bytes 1572872 | tf_op jit(solution)/shard_map/ppermute | solution.py:156
  76.6 29.4 %collective-permute-start.23 = (f32[32,4096]{1,0:T(8,128)}, f32[32,4096]{1,0:T(8,128)}, u32[]{:S(2)}, u32[]{:S(2)}) collective-permute-start(f32[32,4096]{1,0:T(8,128)} %get-tuple-element.89), channel_id=1, source_target_pairs={{0,6},{1,7},{2,0},{3,1},{4,2},{5,3},{6,4},{7,5},{8,14},{9,15},{10,... | collective-permute-start | bytes 1572872 | tf_op jit(solution)/shard_map/ppermute | solution.py:156
  79.4 26.6 %collective-permute-start.24 = (f32[32,4096]{1,0:T(8,128)}, f32[32,4096]{1,0:T(8,128)}, u32[]{:S(2)}, u32[]{:S(2)}) collective-permute-start(f32[32,4096]{1,0:T(8,128)} %get-tuple-element.90), channel_id=1, source_target_pairs={{0,4},{1,5},{2,6},{3,7},{4,0},{5,1},{6,2},{7,3},{8,12},{9,13},{10,... | collective-permute-start | bytes 1572872 | tf_op jit(solution)/shard_map/ppermute | solution.py:156
  87.1 16.7 %collective-permute-start.2 = (f32[32,4096]{1,0:T(8,128)S(1)}, f32[32,4096]{1,0:T(8,128)}, u32[]{:S(2)}, u32[]{:S(2)}) collective-permute-start(f32[32,4096]{1,0:T(8,128)S(1)} %get-tuple-element.27), channel_id=1, source_target_pairs={{0,32},{16,48},{32,64},{48,80},{64,96},{80,112},{96,128},{112,144}... | collective-permute-start | bytes 1572872 | tf_op jit(solution)/shard_map/cond/branch_1_fun/ppermute | solution.py:162
  89.0 14.8 %collective-permute-start.3 = (f32[1]{0:T(128)}, f32[1]{0:T(128)}, u32[]{:S(2)}, u32[]{:S(2)}) collective-permute-start(f32[1]{0:T(128)} %get-tuple-element.28), channel_id=1, source_target_pairs={{0,32},{16,48},{32,64},{48,80},{64,96},{80,112},{96,128},{112,144}... | collective-permute-start | bytes 20 | tf_op jit(solution)/shard_map/cond/branch_1_fun/ppermute | solution.py:162
  103.8 2.2 %copy-start.5 = (f32[1,32,8192]{2,1,0:T(8,128)S(1)}, f32[1,32,8192]{2,1,0:T(8,128)}, u32[]{:S(2)}) copy-start(f32[1,32,8192]{2,1,0:T(8,128)} %param.17) | copy-start | bytes 3145732
  106.0 17.6 %copy-start.6 = (f32[32,4096]{1,0:T(8,128)S(1)}, f32[32,4096]{1,0:T(8,128)}, u32[]{:S(2)}) copy-start(f32[32,4096]{1,0:T(8,128)} %add_multiply_fusion.1) | copy-start | bytes 1572868
  109.4 13.0 %collective-permute-start.9 = (f32[32,4096]{1,0:T(8,128)S(1)}, f32[32,4096]{1,0:T(8,128)}, u32[]{:S(2)}, u32[]{:S(2)}) collective-permute-start(f32[32,4096]{1,0:T(8,128)S(1)} %param.5), channel_id=1, source_target_pairs={{0,32},{16,48},{32,64},{48,80},{64,96},{80,112},{96,128},{112,144}... | collective-permute-start | bytes 1572872 | tf_op jit(solution)/shard_map/cond/branch_1_fun/ppermute | solution.py:162
  (3 other events, 2.6 us)
where the time goes:
time: 127 us; the launch traced here: 126 us
  waiting for transfers between devices  75.5 us (59%)
  starting transfers between devices  19 us (15%)
  Pallas kernels  17.6 us (14%)
  local copies, waits for them, and re-layouts  5.52 us (4%)
  other arithmetic  4.45 us (4%)
  between operations  3.88 us (3%)
    ppermute x6, waiting for transfers between devices, to_x(): lax.ppermute(value, 'fsdp', [(i, i & 9 | ((i >> 1) + by & 3) << 1) for i...  37.5 us
    ppermute x3, waiting for transfers between devices, to_rep(): return lax.ppermute(value, 'rep', [(i, (i + by) % 16) for i in range(16)])  25.8 us
    pallas_call x13, Pallas kernels, call(): pl.pallas_call(wrapped, grid=(width // tile,), in_specs=specs + [ANY] * l...  17.6 us
    ppermute x6, starting transfers between devices, to_x(): lax.ppermute(value, 'fsdp', [(i, i & 9 | ((i >> 1) + by & 3) << 1) for i...  8.97 us
    ppermute x3, waiting for transfers between devices, to_y(): return lax.ppermute(value, 'fsdp', [(i, i ^ 8) for i in range(16)])  8.11 us
    unnamed x22, local copies, waits for them, and re-layouts  5.48 us
    ppermute x3, starting transfers between devices, to_y(): return lax.ppermute(value, 'fsdp', [(i, i ^ 8) for i in range(16)])  4.88 us
    ppermute x4, waiting for transfers between devices, to_core(): return lax.ppermute(value, 'fsdp', [(i, i ^ 1) for i in range(16)])  4.03 us
  transfers between devices with their start and end apart: 16, of which 8 were waited for; matrix products, arithmetic and copies ran while one was open for 2% of the time, Pallas kernels for 11%

commit v1 on v0

v1 whole, which is shorter than its diff:
```python
from functools import partial

import jax
import jax.numpy as jnp
from jax import lax
from jax.experimental import pallas as pl
from jax.experimental.pallas import tpu as pltpu
from jax.sharding import PartitionSpec as P

X_WIDTH = 2560
Y_WIDTH = 3072
HALF = X_WIDTH // 2
TILE = 1024
COST = (0.1, 2, 0.1, 0.1, 0.1, 0.8, 0.01)
LIMIT = 16 * 1024 * 1024
ANY = pl.BlockSpec(memory_space=pl.ANY)
HELD = pl.BlockSpec(memory_space=pltpu.HBM)


def call(kernel, width, tile, ins, outs, after=(), aliases=None, cost=0.1, limit=LIMIT):
    specs, operands = [], []
    for array, start in ins:
        rows, columns = array.shape
        operands.append(array)
        if start is None:
            specs.append(pl.BlockSpec((rows, columns), lambda j: (0, 0)))
        else:
            specs.append(pl.BlockSpec((rows, tile), lambda j, s=start // tile: (0, j + s)))
    out_specs, shapes = [], []
    for rows, columns, start in outs:
        if start is None:
            out_specs.append(pl.BlockSpec((rows, columns), lambda j: (0, 0)))
        else:
            out_specs.append(pl.BlockSpec((rows, tile), lambda j, s=start // tile: (0, j + s)))
        shapes.append(jax.ShapeDtypeStruct((rows, columns), jnp.float32))
    count, skipped = len(ins), len(after)
    pairs = {}
    for out, array in (aliases or {}).items():
        pairs[count + skipped + len(pairs)] = out
    extra = list(after) + list((aliases or {}).values())

    def wrapped(*refs):
        kernel(*refs[:count], *refs[count + len(extra) :])

    return pl.pallas_call(
        wrapped,
        grid=(width // tile,),
        in_specs=specs + [ANY] * skipped + [HELD] * len(pairs),
        out_specs=out_specs,
        out_shape=shapes,
        input_output_aliases=pairs,
        compiler_params=pltpu.CompilerParams(vmem_limit_bytes=limit),
        cost_estimate=pl.CostEstimate(flops=int(cost * 1.15e9), bytes_accessed=int(cost * 3e6), transcendentals=0),
    )(*operands, *extra)


def strips(rows, step, work):
    def one(i, carry):
        work(pl.ds(pl.multiple_of(i * step, step), step))
        return carry

    lax.fori_loop(0, rows // step, one, 0)


def product(cot, acts, start, width, tile, after=()):
    def kernel(c_ref, a_ref, o_ref):
        o_ref[...] = jnp.dot(c_ref[...], a_ref[...], preferred_element_type=jnp.float32)

    return call(kernel, width, tile, [(cot, None), (acts, start)], [(256, width, 0)], after)[0]


def product_add_y(cot, acts, peer, start, after):
    def kernel(c_ref, a_ref, p_ref, stay_ref, go_ref):
        total = jnp.dot(c_ref[...], a_ref[...], preferred_element_type=jnp.float32) + p_ref[...]
        stay_ref[...] = total[:128]
        go_ref[...] = total[128:]

    return call(
        kernel, Y_WIDTH, TILE, [(cot, None), (acts, start), (peer, 0)], [(128, Y_WIDTH, 0)] * 2, after
    )


def product_add_x(cot, acts, peer, start, after):
    def kernel(c_ref, a_ref, p_ref, *o_refs):
        total = jnp.dot(c_ref[...], a_ref[...], preferred_element_type=jnp.float32) + p_ref[...]

        def put(ref, d):
            ref[:32] = total[32 * d : 32 * d + 32]
            ref[32:] = total[128 + 32 * d : 160 + 32 * d]

        put(o_refs[0], 0)
        put(o_refs[1], 1)
        put(o_refs[2], 3)
        for side in range(2):
            pl.when(pl.program_id(0) == side)(partial(put, o_refs[3 + side], 2))

    outs = [(64, X_WIDTH, 0)] * 3 + [(64, HALF, None)] * 2
    return call(kernel, X_WIDTH, HALF, [(cot, None), (acts, start), (peer, 0)], outs, after)


def relay_add(parts, from_left, from_right, after, cost):
    def kernel(a_ref, b_ref, c_ref, d_ref, right_ref, left_ref):
        def work(at):
            right_ref[at] = a_ref[at] + b_ref[at]
            left_ref[at] = c_ref[at] + d_ref[at]

        strips(64, 8, work)

    half = pl.BlockSpec((64, HALF), lambda j: (0, 0))
    other = pl.BlockSpec((64, HALF), lambda j: (0, 1))
    extra = list(after)
    return pl.pallas_call(
        lambda *refs: kernel(*refs[:4], *refs[-2:]),
        grid=(1,),
        in_specs=[half, half, other, half] + [ANY] * len(extra),
        out_specs=[half, other],
        out_shape=[jax.ShapeDtypeStruct((64, X_WIDTH), jnp.float32)] * 2,
        input_output_aliases={0: 0, 2: 1},
        compiler_params=pltpu.CompilerParams(vmem_limit_bytes=LIMIT),
        cost_estimate=pl.CostEstimate(flops=int(cost * 1.15e9), bytes_accessed=int(cost * 3e6), transcendentals=0),
    )(parts[1], from_left, parts[2], from_right, *extra)


def add_split(own, peer, after, cost):
    def kernel(a_ref, b_ref, *o_refs):
        for d in range(4):
            def work(at, d=d):
                from_at = pl.ds(at.start + 32 * d, at.size)
                o_refs[d][at] = a_ref[from_at] + b_ref[from_at]

            strips(32, 8, work)

    return call(
        kernel, Y_WIDTH, TILE, [(own, 0), (peer, 0)], [(32, Y_WIDTH, 0)] * 4, after, cost=cost
    )


def sum_split(terms, after, cost):
    def kernel(a_ref, b_ref, c_ref, *o_refs):
        for i in range(2):
            def work(at, i=i):
                from_at = pl.ds(at.start + 32 * i, at.size)
                o_refs[i][at] = a_ref[from_at] + (b_ref[from_at] + c_ref[from_at])

            strips(32, 8, work)

    return call(kernel, X_WIDTH, HALF, [(t, 0) for t in terms], [(32, X_WIDTH, 0)] * 2, after, cost=cost)


def adam(terms, param, first, second, held, start, tile, whole, after, cost):
    count, columns, width = len(terms), param.shape[1], terms[0].shape[1]

    def kernel(*refs):
        param_ref, first_ref, second_ref = refs[count : count + 3]
        step_ref, new_first_ref, new_second_ref = refs[-3:]

        def work(at):
            grad = refs[0][at]
            for ref in refs[1:count]:
                grad = grad + ref[at]
            new_first = 0.9 * first_ref[at] + 0.1 * grad
            new_second = 0.999 * second_ref[at] + 0.001 * grad * grad
            new_first_ref[at] = new_first
            new_second_ref[at] = new_second
            step_ref[at] = param_ref[at] - 0.1 * (new_first / (jnp.sqrt(new_second) + 1e-08))

        strips(32, 8, work)

    ins = [(t, 0) for t in terms] + [(a, start) for a in (param, first, second)]
    outs = [(32, whole, start if start < whole else 0), (32, columns, start), (32, columns, start)]
    return call(kernel, width, tile, ins, outs, after, held, cost=cost)


def mix(step, peer, held, start, tile, columns):
    def kernel(a_ref, b_ref, o_ref):
        def work(at):
            o_ref[at] = 0.5 * a_ref[at] + 0.5 * b_ref[at]

        strips(32, 8, work)

    return call(
        kernel, step.shape[1], tile, [(step, 0), (peer, 0)], [(32, columns, start)], (),
        None if held is None else {0: held},
    )[0]


def to_core(value):
    return lax.ppermute(value, "fsdp", [(i, i ^ 1) for i in range(16)])


def to_y(value):
    return lax.ppermute(value, "fsdp", [(i, i ^ 8) for i in range(16)])


def to_x(value, by):
    return lax.ppermute(
        value, "fsdp", [(i, (i & 9) | ((((i >> 1) + by) & 3) << 1)) for i in range(16)]
    )


def to_rep(value, by):
    return lax.ppermute(value, "rep", [(i, (i + by) % 16) for i in range(16)])


def dealt(cot):
    me = lax.axis_index("fsdp")
    at = lax.broadcasted_iota(jnp.int32, (512, 512), 0)
    rel = lax.broadcasted_iota(jnp.int32, (512, 512), 1)
    to = rel >> 5
    core = (me ^ 1 ^ (to >> 3)) & 1
    y = ((me >> 3) ^ (to >> 2)) & 1
    x = ((me >> 1) + to) & 3
    source = (y * 8 + x * 2 + core) * 32 + (rel & 31)
    pick = (at == source).astype(cot.dtype)
    return lax.dot_general(
        pick, cot, (((0,), (1,)), ((), ())), preferred_element_type=jnp.float32
    ).astype(cot.dtype)


def push(exponent, values, work, *rest):
    def branch(power, operands):
        got = [to_rep(value, 2**power) for value in operands[0]]
        return got, work(*operands[1])

    return lax.switch(exponent, [partial(branch, p) for p in range(4)], (values, rest))


def body(param, first, second, push_weight, acts, cotangent, exponent):
    cot = dealt(cotangent[0])
    theirs, mine = cot[:256], cot[256:]
    param, first, second, acts = param[0], first[0], second[0], acts[0]
    columns = param.shape[1]
    order = (1, 3, 2)

    b, y = X_WIDTH, 2 * X_WIDTH
    out_y = product(theirs, acts, y, Y_WIDTH, TILE)
    in_y = to_core(out_y)
    out_0 = product(theirs, acts, 0, X_WIDTH, HALF, [out_y])
    in_0 = to_core(out_0)
    out_1 = product(theirs, acts, b, X_WIDTH, HALF, [out_0])
    in_1 = to_core(out_1)
    y_2 = product_add_y(mine, acts, in_y, y, [out_1])
    peer_2 = to_y(y_2[1])
    x_0 = product_add_x(mine, acts, in_0, 0, y_2[:1])
    left_0, right_0 = to_x(x_0[3], 1), to_x(x_0[4], 3)
    x_1 = product_add_x(mine, acts, in_1, b, x_0[:1])
    left_1, right_1 = to_x(x_1[3], 1), to_x(x_1[4], 3)
    both_0 = relay_add(x_0, left_0, right_0, x_1[:1], COST[0])
    from_0 = [to_x(both_0[0], 1), to_x(both_0[1], 3)]
    both_1 = relay_add(x_1, left_1, right_1, both_0[:1], COST[1])
    from_1 = [to_x(both_1[0], 1), to_x(both_1[1], 3)]
    halves_0 = sum_split([x_0[0]] + from_0, both_1[:1], COST[2])
    last_0 = to_y(halves_0[1])
    blocks = add_split(y_2[0], peer_2, halves_0[:1], COST[3])
    last = [to_x(blocks[d], d) for d in order]
    halves_1 = sum_split([x_1[0]] + from_1, blocks[:1], COST[4])
    last_1 = to_y(halves_1[1])
    moments = (param, first, second)
    step, *held = adam(
        [halves_0[0], last_0], *moments, None, 0, X_WIDTH, y, halves_1[:1], COST[5]
    )
    held = {0: step, 1: held[0], 2: held[1]}
    step, *held = adam([halves_1[0], last_1], *moments, held, b, X_WIDTH, y, [], COST[6])
    (got, weight_peer), _ = push(exponent[0], [step, push_weight], lambda: ())
    held = {1: held[0], 2: held[1]}
    step_2, *held = adam([blocks[0]] + last, *moments, held, y, TILE, Y_WIDTH, [got], 1)
    (got_2,), mixed = push(
        exponent[0], [step_2], lambda *v: mix(*v, None, 0, X_WIDTH, columns), step, got
    )
    mixed = mix(step_2, got_2, mixed, y, TILE, columns)
    new_first, new_second = held
    weight = 0.5 * push_weight + 0.5 * weight_peer
    return mixed[None], new_first[None], new_second[None], weight


def solution(mesh):
    return jax.shard_map(
        body,
        mesh=mesh,
        in_specs=(
            P("rep", "fsdp", None),
            P("rep", "fsdp", None),
            P("rep", "fsdp", None),
            P("rep"),
            P("rep", "fsdp", None),
            P("rep", "fsdp", None),
            P(),
        ),
        out_specs=(
            P("rep", "fsdp", None),
            P("rep", "fsdp", None),
            P("rep", "fsdp", None),
            P("rep"),
        ),
        check_vma=False,
    )
```

time: 127 us -> 138 us (1.087)
  starting transfers between devices: 19 us -> 42.2 us
  waiting for transfers between devices: 75.5 us -> 61.4 us
  Pallas kernels: 17.6 us -> 22.1 us
  other arithmetic: 4.45 us -> 0.01 us
    ppermute x6 -> x11, waiting for transfers between devices: 37.5 us -> 23.7 us  [to_x(): lax.ppermute(value, 'fsdp', [(i, i & 9 | ((i >> 1) + by & 3) << 1) for i...]
    ppermute x3, starting transfers between devices: 3.86 us -> 17.2 us  [to_rep(): return lax.ppermute(value, 'rep', [(i, (i + by) % 16) for i in range(16)])]
    ppermute x6 -> x11, starting transfers between devices: 8.97 us -> 18.3 us  [to_x(): lax.ppermute(value, 'fsdp', [(i, i & 9 | ((i >> 1) + by & 3) << 1) for i...]
    ppermute x3, waiting for transfers between devices: 25.8 us -> 30.5 us  [to_rep(): return lax.ppermute(value, 'rep', [(i, (i + by) % 16) for i in range(16)])]
    pallas_call x13 -> x16, Pallas kernels: 17.6 us -> 22.1 us  [the longest x14 21.7 us: call(): pl.pallas_call(wrapped, grid=(width // tile,), in_specs=specs + [ANY] * s...]
    add x2 -> x0, other arithmetic: 3.4 us -> none  [the longest x1 2.14 us: body(): 0.5 * step_x + 0.5 * peer_x]
    ppermute x3, waiting for transfers between devices: 8.11 us -> 4.99 us  [to_y(): return lax.ppermute(value, 'fsdp', [(i, i ^ 8) for i in range(16)])]
    ppermute x4 -> x3, waiting for transfers between devices: 4.03 us -> 2.15 us  [to_core(): return lax.ppermute(value, 'fsdp', [(i, i ^ 1) for i in range(16)])]
  transfers between devices with their start and end apart: 16 -> 20, of which waited for: 8 -> 8; matrix products, arithmetic and copies ran while one was open for 2% -> 0% of each run, Pallas kernels for 11% -> 11%
where the time goes in v1:
time: 138 us; the launch traced here: 137 us
  waiting for transfers between devices  61.4 us (44%)
  starting transfers between devices  42.2 us (31%)
  Pallas kernels  22.1 us (16%)
  local copies, waits for them, and re-layouts  6.61 us (5%)
  between operations  3.87 us (3%)
    ppermute x3, waiting for transfers between devices, to_rep(): return lax.ppermute(value, 'rep', [(i, (i + by) % 16) for i in range(16)])  30.5 us
    ppermute x11, waiting for transfers between devices, to_x(): lax.ppermute(value, 'fsdp', [(i, i & 9 | ((i >> 1) + by & 3) << 1) for i...  23.7 us
    pallas_call x14, Pallas kernels, call(): pl.pallas_call(wrapped, grid=(width // tile,), in_specs=specs + [ANY] * s...  21.7 us
    ppermute x11, starting transfers between devices, to_x(): lax.ppermute(value, 'fsdp', [(i, i & 9 | ((i >> 1) + by & 3) << 1) for i...  18.3 us
    ppermute x3, starting transfers between devices, to_rep(): return lax.ppermute(value, 'rep', [(i, (i + by) % 16) for i in range(16)])  17.2 us
    unnamed x24, local copies, waits for them, and re-layouts  6.57 us
    ppermute x3, starting transfers between devices, to_y(): return lax.ppermute(value, 'fsdp', [(i, i ^ 8) for i in range(16)])  5.98 us
    ppermute x3, waiting for transfers between devices, to_y(): return lax.ppermute(value, 'fsdp', [(i, i ^ 8) for i in range(16)])  4.99 us
  transfers between devices with their start and end apart: 20, of which 8 were waited for; matrix products, arithmetic and copies ran while one was open for 0% of the time, Pallas kernels for 11%

profile of v1, /device:TPU:16, one launch (start us, length us, event | category | flops | bytes accessed | tf_op | source)
XLA Modules:
  0.0 136.7 jit_solution(17561882887642194116)
XLA Ops:
  2.2 2.8 %copy-done.1 = bf16[1,384,8192]{2,1,0:T(8,128)(2,1)S(1)} copy-done((bf16[1,384,8192]{2,1,0:T(8,128)(2,1)S(1)}, bf16[1,384,8192]{2,1,0:T(8,128)(2,1)}, u32[]{:S(2)}) %copy-start.1) | copy-done | bytes 6291480
  10.3 2.1 %collective-permute-done.12.refs_2_ = f32[256,3072]{1,0:T(8,128)S(1)} collective-permute-done((f32[256,3072]{1,0:T(8,128)S(1)}, f32[256,3072]{1,0:T(8,128)S(1)}, u32[]{:S(2)}, u32[]{:S(2)}) %collective-permute-start.12) | collective-permute-done | bytes 3145760 | tf_op jit(solution)/shard_map/ppermute | solution.py:188
  12.4 1.9 %shard_map.105 = (f32[128,3072]{1,0:T(8,128)S(1)}, f32[128,3072]{1,0:T(8,128)S(1)}) custom-call(bf16[256,384]{1,0:T(8,128)(2,1)S(1)} %get-tuple-element.139.refs_0_, bf16[384,8192]{1,0:T(8,128)(2,1)S(1)} %bitcast.16, f32[256,3072]{1,0:T(8,128)S(1)} %collective-permute-done.12.refs_2_, f32[256,2560]{1,0:T(8,128)S(1)} %shard_map.104.refs_3_), custom_call_target="tpu_custom_call" | custom-call | flops 115000000 | bytes 300000 | tf_op jit(solution)/shard_map/pallas_call | solution.py:45
  14.4 2.1 %collective-permute-start.13 = (f32[128,3072]{1,0:T(8,128)S(1)}, f32[128,3072]{1,0:T(8,128)S(1)}, u32[]{:S(2)}, u32[]{:S(2)}) collective-permute-start(f32[128,3072]{1,0:T(8,128)S(1)} %get-tuple-element.102), channel_id=1, source_target_pairs={{0,8},{1,9},{2,10},{3,11},{4,12},{5,13},{6,14},{7,15},{8,0},{9,1},... | collective-permute-start | bytes 4718600 | tf_op jit(solution)/shard_map/ppermute | solution.py:192
  19.4 2.1 %collective-permute-start.16 = (f32[64,1280]{1,0:T(8,128)S(1)}, f32[64,1280]{1,0:T(8,128)S(1)}, u32[]{:S(2)}, u32[]{:S(2)}) collective-permute-start(f32[64,1280]{1,0:T(8,128)S(1)} %get-tuple-element.107), channel_id=1, source_target_pairs={{0,6},{1,7},{2,0},{3,1},{4,2},{5,3},{6,4},{7,5},{8,14},{9,15},{10,... | collective-permute-start | bytes 983048 | tf_op jit(solution)/shard_map/ppermute | solution.py:196
  23.2 3.2 %collective-permute-start.21 = (f32[64,1280]{1,0:T(8,128)S(1)}, f32[64,1280]{1,0:T(8,128)S(1)}, u32[]{:S(2)}, u32[]{:S(2)}) collective-permute-start(f32[64,1280]{1,0:T(8,128)S(1)} %get-tuple-element.114), channel_id=1, source_target_pairs={{0,6},{1,7},{2,0},{3,1},{4,2},{5,3},{6,4},{7,5},{8,14},{9,15},{10,... | collective-permute-start | bytes 983048 | tf_op jit(solution)/shard_map/ppermute | solution.py:196
  26.4 3.6 %collective-permute-done.15.refs_1_ = f32[64,1280]{1,0:T(8,128)S(1)} collective-permute-done((f32[64,1280]{1,0:T(8,128)S(1)}, f32[64,1280]{1,0:T(8,128)S(1)}, u32[]{:S(2)}, u32[]{:S(2)}) %collective-permute-start.15) | collective-permute-done | bytes 327712 | tf_op jit(solution)/shard_map/ppermute | solution.py:196
  31.7 2.0 %collective-permute-start.19 = (f32[64,2560]{1,0:T(8,128)S(1)}, f32[64,2560]{1,0:T(8,128)S(1)}, u32[]{:S(2)}, u32[]{:S(2)}) collective-permute-start(f32[64,2560]{1,0:T(8,128)S(1)} %get-tuple-element.110), channel_id=1, source_target_pairs={{0,6},{1,7},{2,0},{3,1},{4,2},{5,3},{6,4},{7,5},{8,14},{9,15},{10,... | collective-permute-start | bytes 1966088 | tf_op jit(solution)/shard_map/ppermute | solution.py:196
  33.7 3.4 %collective-permute-done.20.refs_1_ = f32[64,1280]{1,0:T(8,128)S(1)} collective-permute-done((f32[64,1280]{1,0:T(8,128)S(1)}, f32[64,1280]{1,0:T(8,128)S(1)}, u32[]{:S(2)}, u32[]{:S(2)}) %collective-permute-start.20) | collective-permute-done | bytes 327712 | tf_op jit(solution)/shard_map/ppermute | solution.py:196
  38.9 2.0 %collective-permute-start.26 = (f32[64,2560]{1,0:T(8,128)S(1)}, f32[64,2560]{1,0:T(8,128)S(1)}, u32[]{:S(2)}, u32[]{:S(2)}) collective-permute-start(f32[64,2560]{1,0:T(8,128)S(1)} %get-tuple-element.121), channel_id=1, source_target_pairs={{0,6},{1,7},{2,0},{3,1},{4,2},{5,3},{6,4},{7,5},{8,14},{9,15},{10,... | collective-permute-start | bytes 1966088 | tf_op jit(solution)/shard_map/ppermute | solution.py:196
  40.9 10.2 %collective-permute-done.18.refs_1_ = f32[64,2560]{1,0:T(8,128)S(1)} collective-permute-done((f32[64,2560]{1,0:T(8,128)S(1)}, f32[64,2560]{1,0:T(8,128)S(1)}, u32[]{:S(2)}, u32[]{:S(2)}) %collective-permute-start.18) | collective-permute-done | bytes 655392 | tf_op jit(solution)/shard_map/ppermute | solution.py:196
  53.5 2.0 %shard_map.111 = (f32[32,3072]{1,0:T(8,128)S(1)}, f32[32,3072]{1,0:T(8,128)}, f32[32,3072]{1,0:T(8,128)}, f32[32,3072]{1,0:T(8,128)}) custom-call(f32[128,3072]{1,0:T(8,128)S(1)} %get-tuple-element.101.refs_3_.refs_0_, f32[128,3072]{1,0:T(8,128)S(1)} %collective-permute-done.13.refs_1_, f32[32,2560]{1,0:T(8,128)S(1)} %get-tuple-element.116.refs_2_.refs_0_), custom_call_target="tpu_custom_call" | custom-call | flops 115000000 | bytes 300000 | tf_op jit(solution)/shard_map/pallas_call | solution.py:45
  58.7 6.5 %collective-permute-done.25.refs_1_ = f32[64,2560]{1,0:T(8,128)S(1)} collective-permute-done((f32[64,2560]{1,0:T(8,128)S(1)}, f32[64,2560]{1,0:T(8,128)S(1)}, u32[]{:S(2)}, u32[]{:S(2)}) %collective-permute-start.25) | collective-permute-done | bytes 655392 | tf_op jit(solution)/shard_map/ppermute | solution.py:196
  67.0 2.0 %collective-permute-start.27 = (f32[32,2560]{1,0:T(8,128)S(1)}, f32[32,2560]{1,0:T(8,128)S(1)}, u32[]{:S(2)}, u32[]{:S(2)}) collective-permute-start(f32[32,2560]{1,0:T(8,128)S(1)} %get-tuple-element.123), channel_id=1, source_target_pairs={{0,8},{1,9},{2,10},{3,11},{4,12},{5,13},{6,14},{7,15},{8,0},{9,1},... | collective-permute-start | bytes 983048 | tf_op jit(solution)/shard_map/ppermute | solution.py:192
  71.5 5.0 %collective-permute-done.27.refs_1_ = f32[32,2560]{1,0:T(8,128)S(1)} collective-permute-done((f32[32,2560]{1,0:T(8,128)S(1)}, f32[32,2560]{1,0:T(8,128)S(1)}, u32[]{:S(2)}, u32[]{:S(2)}) %collective-permute-start.27) | collective-permute-done | bytes 327712 | tf_op jit(solution)/shard_map/ppermute | solution.py:192
  78.5 24.9 %conditional.2 = (f32[32,5120]{1,0:T(8,128)}, f32[1]{0:T(128)}) conditional(s32[]{:T(128)} %bitcast.5, (f32[32,5120]{1,0:T(8,128)S(1)}, f32[1]{0:T(128)}) %tuple.40, (f32[32,5120]{1,0:T(8,128)S(1)}, f32[1]{0:T(128)}) %tuple.40, (f32[32,5120]{1,0:T(8,128)S(1)}, f32[1]{0:T(128)}) %tuple.40, (f32[32,5120]{1,0:T(8,128)S(1)}, ...), branch_computations={%region_0.0_spmd, %region_1.0_spmd, %region_2.0_spmd, %region_3.0_... | conditional | bytes 2621552 | solution.py:225
  78.5 3.3 %collective-permute-start.4 = (f32[32,5120]{1,0:T(8,128)S(1)}, f32[32,5120]{1,0:T(8,128)}, u32[]{:S(2)}, u32[]{:S(2)}) collective-permute-start(f32[32,5120]{1,0:T(8,128)S(1)} %get-tuple-element.44), channel_id=1, source_target_pairs={{0,64},{16,80},{32,96},{48,112},{64,128},{80,144},{96,160},{112,17... | collective-permute-start | bytes 1966088 | tf_op jit(solution)/shard_map/cond/branch_2_fun/ppermute | solution.py:202
  81.8 4.5 %collective-permute-start.5 = (f32[1]{0:T(128)}, f32[1]{0:T(128)}, u32[]{:S(2)}, u32[]{:S(2)}) collective-permute-start(f32[1]{0:T(128)} %get-tuple-element.45), channel_id=1, source_target_pairs={{0,64},{16,80},{32,96},{48,112},{64,128},{80,144},{96,160},{112,17... | collective-permute-start | bytes 20 | tf_op jit(solution)/shard_map/cond/branch_2_fun/ppermute | solution.py:202
  86.2 17.1 %collective-permute-done.5 = f32[1]{0:T(128)} collective-permute-done((f32[1]{0:T(128)}, f32[1]{0:T(128)}, u32[]{:S(2)}, u32[]{:S(2)}) %collective-permute-start.5) | collective-permute-done | bytes 36 | tf_op jit(solution)/shard_map/cond/branch_2_fun/ppermute | solution.py:202
  105.0 3.5 %shard_map.115 = (f32[32,3072]{1,0:T(8,128)}, f32[32,8192]{1,0:T(8,128)}, f32[32,8192]{1,0:T(8,128)}) custom-call(f32[32,3072]{1,0:T(8,128)S(1)} %copy-done.6, f32[32,3072]{1,0:T(8,128)} %collective-permute-done.22.refs_1_, f32[32,3072]{1,0:T(8,128)} %collective-permute-done.23.refs_2_, ...), custom_call_target="tpu_custom_call", output_to_operand_aliasing={{1}: (8, {}), {2}: (9, {})} | custom-call | flops 1150000000 | bytes 3000000 | tf_op jit(solution)/shard_map/pallas_call | solution.py:45
  108.5 24.0 %conditional.3 = (f32[32,3072]{1,0:T(8,128)}, f32[32,8192]{1,0:T(8,128)S(1)}) conditional(s32[]{:T(128)} %bitcast.5, (f32[32,3072]{1,0:T(8,128)}, f32[32,5120]{1,0:T(8,128)S(1)}, f32[32,5120]{1,0:T(8,128)}) %tuple.52, (f32[32,3072]{1,0:T(8,128)}, f32[32,5120]{1,0:T(8,128)S(1)}, f32[32,5120]{1,0:T(8,128)}) %tuple.53, ...), branch_computations={%region_4.0_spmd, %region_5.0_spmd, %region_6.0_spmd, %region_7.0_... | conditional | flops 115000000 | bytes 1872920 | solution.py:225
  108.5 9.4 %collective-permute-start.10 = (f32[32,3072]{1,0:T(8,128)}, f32[32,3072]{1,0:T(8,128)}, u32[]{:S(2)}, u32[]{:S(2)}) collective-permute-start(f32[32,3072]{1,0:T(8,128)} %get-tuple-element.54), channel_id=1, source_target_pairs={{0,64},{16,80},{32,96},{48,112},{64,128},{80,144},{96,160},{112,17... | collective-permute-start | bytes 1179656 | tf_op jit(solution)/shard_map/cond/branch_2_fun/ppermute | solution.py:202
  119.2 13.3 %collective-permute-done.10 = f32[32,3072]{1,0:T(8,128)} collective-permute-done((f32[32,3072]{1,0:T(8,128)}, f32[32,3072]{1,0:T(8,128)}, u32[]{:S(2)}, u32[]{:S(2)}) %collective-permute-start.10) | collective-permute-done | bytes 393248 | tf_op jit(solution)/shard_map/cond/branch_2_fun/ppermute | solution.py:202
  132.5 2.1 %shard_map.116 = f32[32,8192]{1,0:T(8,128)S(1)} custom-call(f32[32,3072]{1,0:T(8,128)} %get-tuple-element.132.refs_0_, f32[32,3072]{1,0:T(8,128)} %get-tuple-element.133.refs_1_, f32[32,8192]{1,0:T(8,128)S(1)} %get-tuple-element.134.refs_2_), custom_call_target="tpu_custom_call", output_to_operand_aliasing={{}: (2, {})} | custom-call | flops 115000000 | bytes 300000 | tf_op jit(solution)/shard_map/pallas_call | solution.py:45
  (62 shorter events, 28.7 us)
Async XLA Ops:
  6.7 5.7 %collective-permute-start.12 = (f32[256,3072]{1,0:T(8,128)S(1)}, f32[256,3072]{1,0:T(8,128)S(1)}, u32[]{:S(2)}, u32[]{:S(2)}) collective-permute-start(f32[256,3072]{1,0:T(8,128)S(1)} %shard_map.102.refs_2_), channel_id=1, source_target_pairs={{0,1},{1,0},{2,3},{3,2},{4,5},{5,4},{6,7},{7,6},{8,9},{9,8},{10,11... | collective-permute-start | bytes 9437192 | tf_op jit(solution)/shard_map/ppermute | solution.py:188
  8.2 8.3 %collective-permute-start.14 = (f32[256,2560]{1,0:T(8,128)S(1)}, f32[256,2560]{1,0:T(8,128)S(1)}, u32[]{:S(2)}, u32[]{:S(2)}) collective-permute-start(f32[256,2560]{1,0:T(8,128)S(1)} %shard_map.103.refs_2_), channel_id=1, source_target_pairs={{0,1},{1,0},{2,3},{3,2},{4,5},{5,4},{6,7},{7,6},{8,9},{9,8},{10,11... | collective-permute-start | bytes 7864328 | tf_op jit(solution)/shard_map/ppermute | solution.py:188
  10.2 11.3 %collective-permute-start.17 = (f32[256,2560]{1,0:T(8,128)S(1)}, f32[256,2560]{1,0:T(8,128)S(1)}, u32[]{:S(2)}, u32[]{:S(2)}) collective-permute-start(f32[256,2560]{1,0:T(8,128)S(1)} %shard_map.104.refs_3_), channel_id=1, source_target_pairs={{0,1},{1,0},{2,3},{3,2},{4,5},{5,4},{6,7},{7,6},{8,9},{9,8},{10,11... | collective-permute-start | bytes 7864328 | tf_op jit(solution)/shard_map/ppermute | solution.py:188
  14.4 39.1 %collective-permute-start.13 = (f32[128,3072]{1,0:T(8,128)S(1)}, f32[128,3072]{1,0:T(8,128)S(1)}, u32[]{:S(2)}, u32[]{:S(2)}) collective-permute-start(f32[128,3072]{1,0:T(8,128)S(1)} %get-tuple-element.102), channel_id=1, source_target_pairs={{0,8},{1,9},{2,10},{3,11},{4,12},{5,13},{6,14},{7,15},{8,0},{9,1},... | collective-permute-start | bytes 4718600 | tf_op jit(solution)/shard_map/ppermute | solution.py:192
  18.2 11.9 %collective-permute-start.15 = (f32[64,1280]{1,0:T(8,128)S(1)}, f32[64,1280]{1,0:T(8,128)S(1)}, u32[]{:S(2)}, u32[]{:S(2)}) collective-permute-start(f32[64,1280]{1,0:T(8,128)S(1)} %get-tuple-element.105), channel_id=1, source_target_pairs={{0,2},{1,3},{2,4},{3,5},{4,6},{5,7},{6,0},{7,1},{8,10},{9,11},{10,... | collective-permute-start | bytes 983048 | tf_op jit(solution)/shard_map/ppermute | solution.py:196
  19.4 10.7 %collective-permute-start.16 = (f32[64,1280]{1,0:T(8,128)S(1)}, f32[64,1280]{1,0:T(8,128)S(1)}, u32[]{:S(2)}, u32[]{:S(2)}) collective-permute-start(f32[64,1280]{1,0:T(8,128)S(1)} %get-tuple-element.107), channel_id=1, source_target_pairs={{0,6},{1,7},{2,0},{3,1},{4,2},{5,3},{6,4},{7,5},{8,14},{9,15},{10,... | collective-permute-start | bytes 983048 | tf_op jit(solution)/shard_map/ppermute | solution.py:196
  23.1 13.9 %collective-permute-start.20 = (f32[64,1280]{1,0:T(8,128)S(1)}, f32[64,1280]{1,0:T(8,128)S(1)}, u32[]{:S(2)}, u32[]{:S(2)}) collective-permute-start(f32[64,1280]{1,0:T(8,128)S(1)} %get-tuple-element.112), channel_id=1, source_target_pairs={{0,2},{1,3},{2,4},{3,5},{4,6},{5,7},{6,0},{7,1},{8,10},{9,11},{10,... | collective-permute-start | bytes 983048 | tf_op jit(solution)/shard_map/ppermute | solution.py:196
  23.2 13.9 %collective-permute-start.21 = (f32[64,1280]{1,0:T(8,128)S(1)}, f32[64,1280]{1,0:T(8,128)S(1)}, u32[]{:S(2)}, u32[]{:S(2)}) collective-permute-start(f32[64,1280]{1,0:T(8,128)S(1)} %get-tuple-element.114), channel_id=1, source_target_pairs={{0,6},{1,7},{2,0},{3,1},{4,2},{5,3},{6,4},{7,5},{8,14},{9,15},{10,... | collective-permute-start | bytes 983048 | tf_op jit(solution)/shard_map/ppermute | solution.py:196
  30.2 20.9 %collective-permute-start.18 = (f32[64,2560]{1,0:T(8,128)S(1)}, f32[64,2560]{1,0:T(8,128)S(1)}, u32[]{:S(2)}, u32[]{:S(2)}) collective-permute-start(f32[64,2560]{1,0:T(8,128)S(1)} %get-tuple-element.109.refs_4_), channel_id=1, source_target_pairs={{0,2},{1,3},{2,4},{3,5},{4,6},{5,7},{6,0},{7,1},{8,10},{9,11},{10,... | collective-permute-start | bytes 1966088 | tf_op jit(solution)/shard_map/ppermute | solution.py:196
  31.7 19.4 %collective-permute-start.19 = (f32[64,2560]{1,0:T(8,128)S(1)}, f32[64,2560]{1,0:T(8,128)S(1)}, u32[]{:S(2)}, u32[]{:S(2)}) collective-permute-start(f32[64,2560]{1,0:T(8,128)S(1)} %get-tuple-element.110), channel_id=1, source_target_pairs={{0,6},{1,7},{2,0},{3,1},{4,2},{5,3},{6,4},{7,5},{8,14},{9,15},{10,... | collective-permute-start | bytes 1966088 | tf_op jit(solution)/shard_map/ppermute | solution.py:196
  37.2 27.9 %collective-permute-start.25 = (f32[64,2560]{1,0:T(8,128)S(1)}, f32[64,2560]{1,0:T(8,128)S(1)}, u32[]{:S(2)}, u32[]{:S(2)}) collective-permute-start(f32[64,2560]{1,0:T(8,128)S(1)} %get-tuple-element.115.refs_3_), channel_id=1, source_target_pairs={{0,2},{1,3},{2,4},{3,5},{4,6},{5,7},{6,0},{7,1},{8,10},{9,11},{10,... | collective-permute-start | bytes 1966088 | tf_op jit(solution)/shard_map/ppermute | solution.py:196
  38.9 27.6 %collective-permute-start.26 = (f32[64,2560]{1,0:T(8,128)S(1)}, f32[64,2560]{1,0:T(8,128)S(1)}, u32[]{:S(2)}, u32[]{:S(2)}) collective-permute-start(f32[64,2560]{1,0:T(8,128)S(1)} %get-tuple-element.121), channel_id=1, source_target_pairs={{0,6},{1,7},{2,0},{3,1},{4,2},{5,3},{6,4},{7,5},{8,14},{9,15},{10,... | collective-permute-start | bytes 1966088 | tf_op jit(solution)/shard_map/ppermute | solution.py:196
  51.6 18.7 %collective-permute-start.28 = (f32[32,2560]{1,0:T(8,128)S(1)}, f32[32,2560]{1,0:T(8,128)S(1)}, u32[]{:S(2)}, u32[]{:S(2)}) collective-permute-start(f32[32,2560]{1,0:T(8,128)S(1)} %get-tuple-element.124), channel_id=1, source_target_pairs={{0,8},{1,9},{2,10},{3,11},{4,12},{5,13},{6,14},{7,15},{8,0},{9,1},... | collective-permute-start | bytes 983048 | tf_op jit(solution)/shard_map/ppermute | solution.py:192
  53.4 16.8 %copy-start.2 = (f32[1,32,8192]{2,1,0:T(8,128)S(1)}, f32[1,32,8192]{2,1,0:T(8,128)}, u32[]{:S(2)}) copy-start(f32[1,32,8192]{2,1,0:T(8,128)} %param.15) | copy-start | bytes 3145732
  53.4 16.8 %copy-start.3 = (f32[1,32,8192]{2,1,0:T(8,128)S(1)}, f32[1,32,8192]{2,1,0:T(8,128)}, u32[]{:S(2)}) copy-start(f32[1,32,8192]{2,1,0:T(8,128)} %param.16) | copy-start | bytes 3145732
  53.4 16.9 %copy-start.4 = (f32[1,32,8192]{2,1,0:T(8,128)S(1)}, f32[1,32,8192]{2,1,0:T(8,128)}, u32[]{:S(2)}) copy-start(f32[1,32,8192]{2,1,0:T(8,128)} %param.17) | copy-start | bytes 3145732
  55.4 16.0 %copy-start.5 = (f32[32,3072]{1,0:T(8,128)}, f32[32,3072]{1,0:T(8,128)S(1)}, u32[]{:S(2)}) copy-start(f32[32,3072]{1,0:T(8,128)S(1)} %get-tuple-element.117.refs_3_.refs_0_) | copy-start | bytes 1179652
  55.4 48.5 %collective-permute-start.22 = (f32[32,3072]{1,0:T(8,128)}, f32[32,3072]{1,0:T(8,128)}, u32[]{:S(2)}, u32[]{:S(2)}) collective-permute-start(f32[32,3072]{1,0:T(8,128)} %get-tuple-element.118), channel_id=1, source_target_pairs={{0,2},{1,3},{2,4},{3,5},{4,6},{5,7},{6,0},{7,1},{8,10},{9,11},{10,... | collective-permute-start | bytes 1179656 | tf_op jit(solution)/shard_map/ppermute | solution.py:196
  56.9 47.1 %collective-permute-start.23 = (f32[32,3072]{1,0:T(8,128)}, f32[32,3072]{1,0:T(8,128)}, u32[]{:S(2)}, u32[]{:S(2)}) collective-permute-start(f32[32,3072]{1,0:T(8,128)} %get-tuple-element.119), channel_id=1, source_target_pairs={{0,6},{1,7},{2,0},{3,1},{4,2},{5,3},{6,4},{7,5},{8,14},{9,15},{10,... | collective-permute-start | bytes 1179656 | tf_op jit(solution)/shard_map/ppermute | solution.py:196
  65.1 38.8 %collective-permute-start.24 = (f32[32,3072]{1,0:T(8,128)}, f32[32,3072]{1,0:T(8,128)}, u32[]{:S(2)}, u32[]{:S(2)}) collective-permute-start(f32[32,3072]{1,0:T(8,128)} %get-tuple-element.120), channel_id=1, source_target_pairs={{0,4},{1,5},{2,6},{3,7},{4,0},{5,1},{6,2},{7,3},{8,12},{9,13},{10,... | collective-permute-start | bytes 1179656 | tf_op jit(solution)/shard_map/ppermute | solution.py:196
  67.0 9.4 %collective-permute-start.27 = (f32[32,2560]{1,0:T(8,128)S(1)}, f32[32,2560]{1,0:T(8,128)S(1)}, u32[]{:S(2)}, u32[]{:S(2)}) collective-permute-start(f32[32,2560]{1,0:T(8,128)S(1)} %get-tuple-element.123), channel_id=1, source_target_pairs={{0,8},{1,9},{2,10},{3,11},{4,12},{5,13},{6,14},{7,15},{8,0},{9,1},... | collective-permute-start | bytes 983048 | tf_op jit(solution)/shard_map/ppermute | solution.py:192
  78.5 24.9 %collective-permute-start.4 = (f32[32,5120]{1,0:T(8,128)S(1)}, f32[32,5120]{1,0:T(8,128)}, u32[]{:S(2)}, u32[]{:S(2)}) collective-permute-start(f32[32,5120]{1,0:T(8,128)S(1)} %get-tuple-element.44), channel_id=1, source_target_pairs={{0,64},{16,80},{32,96},{48,112},{64,128},{80,144},{96,160},{112,17... | collective-permute-start | bytes 1966088 | tf_op jit(solution)/shard_map/cond/branch_2_fun/ppermute | solution.py:202
  81.8 21.6 %collective-permute-start.5 = (f32[1]{0:T(128)}, f32[1]{0:T(128)}, u32[]{:S(2)}, u32[]{:S(2)}) collective-permute-start(f32[1]{0:T(128)} %get-tuple-element.45), channel_id=1, source_target_pairs={{0,64},{16,80},{32,96},{48,112},{64,128},{80,144},{96,160},{112,17... | collective-permute-start | bytes 20 | tf_op jit(solution)/shard_map/cond/branch_2_fun/ppermute | solution.py:202
  108.5 24.0 %collective-permute-start.10 = (f32[32,3072]{1,0:T(8,128)}, f32[32,3072]{1,0:T(8,128)}, u32[]{:S(2)}, u32[]{:S(2)}) collective-permute-start(f32[32,3072]{1,0:T(8,128)} %get-tuple-element.54), channel_id=1, source_target_pairs={{0,64},{16,80},{32,96},{48,112},{64,128},{80,144},{96,160},{112,17... | collective-permute-start | bytes 1179656 | tf_op jit(solution)/shard_map/cond/branch_2_fun/ppermute | solution.py:202
  (8 other events, 23.3 us)
